TPU v7x, 32 devices: a whole 2x2x4 slice. The times are simulated.
32 devices in a mesh: branch: 4 (over y, x), row: 8 (over z, core).
Axes of the slice: x: 2, y: 2, z: 4, core: 2. Of those that a mesh axis runs over, the one named last changes fastest.
Arguments:
- root_cov: bfloat16 [2304, 2304], P('row', 'branch')
- diag_factor: float32 [4, 3, 576, 576], P('branch')
- panel_factor: float32 [4, 3, 2304, 576], P('branch', None, 'row'), may hold values from -0.009765625 to 0.009765625
- chain_factor: float32 [4, 2, 576, 576], P('branch'), may hold values from -0.25 to 0.25
- panel_tiles: int32 [4, 3], P('branch'), may hold values from 0 to 3, as said below
Outputs:
- panel_cov: float32 [4, 3, 2304, 576], P('branch', None, 'row')
- block_cov: float32 [4, 5, 576, 576], P('branch')
Inputs may be any that keep to these rules, and one draw needn't show every extreme that they name: `panel_tiles`: the entries of a row are distinct; the first 2 and the first 1 entries of a row are the level-two and level-three patterns.
All inputs are finite; a program needn't handle non-finite values.
Results may differ from a plain program's by a relative error of at most 0.0029.
Values may be sent and summed in bfloat16 or wider, within the bound.
A program may use at most 192 MiB of HBM per device.

v0:
```python
import jax
import jax.numpy as jnp
from jax import lax
from jax.sharding import PartitionSpec as P

HIGHEST = lax.Precision.HIGHEST


def product(left_mat, right_mat):
    return jnp.dot(left_mat, right_mat, precision=HIGHEST, preferred_element_type=jnp.float32)


def on_device(root_cov, diag_factor, panel_factor, chain_factor, panel_tiles):
    node_width = diag_factor.shape[-1]
    rows_here = panel_factor.shape[2]
    per_tile = node_width // rows_here
    tile_total = lax.axis_size("row") // per_tile
    counts = (3 * tile_total // 4, tile_total // 2, tile_total // 4)
    root_rows = lax.all_gather(root_cov, "branch", axis=1, tiled=True)
    my_tile = lax.axis_index("row") // per_tile
    identity = jnp.eye(node_width, dtype=jnp.float32)
    panels = []
    blocks = []
    crosses = []
    for layer_index in range(3):
        inverse = jax.scipy.linalg.solve_triangular(
            diag_factor[0, layer_index], identity, lower=True
        )
        gram = product(inverse.T, inverse)
        chosen = jnp.any(panel_tiles[0, : counts[layer_index]] == my_tile)
        scaled = jnp.where(chosen, product(panel_factor[0, layer_index], inverse), 0.0)
        gathered = jnp.dot(
            root_rows,
            lax.all_gather(scaled.astype(jnp.bfloat16), "row", axis=0, tiled=True),
            preferred_element_type=jnp.float32,
        )
        if layer_index == 0:
            panel = -jnp.where(chosen, gathered, 0.0)
            block = gram - lax.psum(product(scaled.T, panel), "row")
        else:
            previous_panel = panels[-1]
            previous_block = blocks[-1]
            scaled_chain = product(chain_factor[0, layer_index - 1], inverse)
            panel = -jnp.where(chosen, gathered + product(previous_panel, scaled_chain), 0.0)
            cross_sum, block_sum = lax.psum(
                (product(previous_panel.T, scaled), product(scaled.T, panel)), "row"
            )
            cross = -(cross_sum + product(previous_block, scaled_chain))
            block = gram - block_sum - product(scaled_chain.T, cross)
            crosses.append(cross)
        panels.append(panel)
        blocks.append(block)
    return (jnp.stack(panels)[None], jnp.stack(blocks + crosses)[None])


def solution(mesh):
    in_specs = (
        P("row", "branch"),
        P("branch", None, None, None),
        P("branch", None, "row", None),
        P("branch", None, None, None),
        P("branch", None),
    )
    out_specs = (P("branch", None, "row", None), P("branch", None, None, None))
    return jax.shard_map(
        on_device, mesh=mesh, in_specs=in_specs, out_specs=out_specs, check_vma=False
    )
```

profile of v0, /device:TPU:0, one launch (start us, length us, event | category | flops | bytes accessed | tf_op | source)
XLA Modules:
  0.0 502.8 jit_solution(1767455906042671020)
XLA Ops:
  8.1 4.2 bitcast_select_fusion.2
  13.5 11.7 %while.6 = (s32[]{:T(128)}, f32[576,576]{1,0:T(8,128)}, s32[4,2]{0,1:T(2,128)S(1)}, f32[4,128,128]{2,1,0:T(8,128)S(1)}, s32[]{:T(128)}) while((s32[]{:T(128)}, f32[576,576]{1,0:T(8,128)}, s32[4,2]{0,1:T(2,128)S(1)}, f32[4,128,128]{2,1,0:T(8,128)S(1)}, s32[]{:T(128)}) %tuple.93), condition=%wide.while_cond, body=%wide.while_body.sunk | while | flops 2 | bytes 131189 | solution.py:26
  26.6 11.7 %while.7 = (s32[]{:T(128)}, f32[576,576]{1,0:T(8,128)}, s32[4,2]{0,1:T(2,128)S(1)}, f32[4,128,128]{2,1,0:T(8,128)S(1)}, s32[]{:T(128)}) while((s32[]{:T(128)}, f32[576,576]{1,0:T(8,128)}, s32[4,2]{0,1:T(2,128)S(1)}, f32[4,128,128]{2,1,0:T(8,128)S(1)}, s32[]{:T(128)}) %tuple.94), condition=%wide.while_cond.clone, body=%wide.while_body.clone.sunk | while | flops 2 | bytes 131189 | solution.py:26
  40.6 50.6 %custom-call.5 = f32[5,128,128]{1,2,0:T(8,128)} custom-call(f32[5,128,128]{2,1,0:T(8,128)} %get-tuple-element.95), custom_call_target="InvertDiagBlocksLowerTriangular" | custom-call | tf_op jit(solution)/shard_map/jit(_solve_triangular)/triangular_solve | solution.py:26
  102.2 4.1 convolution_select_fusion.2
  108.3 49.9 %custom-call.6 = f32[5,128,128]{1,2,0:T(8,128)S(1)} custom-call(f32[5,128,128]{2,1,0:T(8,128)} %get-tuple-element.96), custom_call_target="InvertDiagBlocksLowerTriangular" | custom-call | tf_op jit(solution)/shard_map/jit(_solve_triangular)/triangular_solve | solution.py:26
  167.6 4.1 convolution_select_fusion.1
  173.0 11.8 %while.8 = (s32[]{:T(128)}, f32[576,576]{1,0:T(8,128)}, s32[4,2]{0,1:T(2,128)S(1)}, f32[4,128,128]{2,1,0:T(8,128)S(1)}, s32[]{:T(128)}) while((s32[]{:T(128)}, f32[576,576]{1,0:T(8,128)}, s32[4,2]{0,1:T(2,128)S(1)}, f32[4,128,128]{2,1,0:T(8,128)S(1)}, s32[]{:T(128)}) %tuple.95), condition=%wide.while_cond.clone.1, body=%wide.while_body.clone.1.sunk | while | flops 2 | bytes 131189 | solution.py:26
  184.8 49.1 %custom-call.7 = f32[5,128,128]{1,2,0:T(8,128)S(1)} custom-call(f32[5,128,128]{2,1,0:T(8,128)S(1)} %pad_maximum_fusion.2), custom_call_target="InvertDiagBlocksLowerTriangular" | custom-call | tf_op jit(solution)/shard_map/jit(_solve_triangular)/triangular_solve | solution.py:26
  243.9 3.4 convolution_select_fusion
  249.2 6.8 %fusion.2 = f32[576,576]{1,0:T(8,128)} fusion(f32[576,576]{0,1:T(8,128)S(1)} %convolution_dynamic-update-slice_fusion.1, f32[1,2,576,576]{3,2,1,0:T(8,128)} %param.10), kind=kOutput, calls=%fused_computation.15 | convolution fusion | flops 2293235712 | bytes 4128768 | tf_op jit(solution)/shard_map/dot_general | solution.py:10
  256.0 5.3 %fusion = f32[576,576]{1,0:T(8,128)} fusion(f32[576,576]{0,1:T(8,128)S(1)} %convolution_dynamic-update-slice_fusion, f32[1,2,576,576]{3,2,1,0:T(8,128)S(1)} %copy-done.26), kind=kOutput, calls=%fused_computation.12 | convolution fusion | flops 2293235712 | bytes 4276224 | tf_op jit(solution)/shard_map/dot_general | solution.py:10
  261.3 3.2 copy.16
  264.6 4.0 reshape.47
  268.7 4.2 fusion.11
  273.8 3.9 fusion.117
  277.7 3.6 convolution_bitcast_fusion.1
  281.3 3.0 fusion.10
  284.4 3.9 fusion.123
  288.3 4.3 fusion.119
  292.6 3.9 fusion.120
  296.5 3.6 convolution_bitcast_fusion
  303.3 3.9 fusion.122
  307.2 5.5 %fusion.118 = f32[576,576]{1,0:T(8,128)} fusion(f32[576,576]{0,1:T(8,128)S(1)} %convolution_dynamic-update-slice_fusion.1), kind=kOutput, calls=%fused_computation.195 | convolution fusion | flops 2293235712 | bytes 2654208 | tf_op jit(solution)/shard_map/dot_general | solution.py:10
  312.6 5.3 %fusion.121 = f32[576,576]{1,0:T(8,128)} fusion(f32[576,576]{0,1:T(8,128)S(1)} %convolution_dynamic-update-slice_fusion), kind=kOutput, calls=%fused_computation.198 | convolution fusion | flops 2293235712 | bytes 2654208 | tf_op jit(solution)/shard_map/dot_general | solution.py:10
  319.5 148.9 %all-reduce.5.cloned.1.call-done = (f32[576,576]{1,0:T(8,128)}, f32[576,576]{1,0:T(8,128)}, f32[576,576]{1,0:T(8,128)}, f32[576,576]{1,0:T(8,128)}, f32[576,576]{1,0:T(8,128)}) async-done(((f32[576,576]{1,0:T(8,128)}, f32[576,576]{1,0:T(8,128)}, f32[576,576]{1,0:T(8,128)}, f32[576,576]{1,0:T(8,128)}, f32[576,576]{1,0:T(8,128)}), (f32[576,576]{1,0:T(8,128)}, f32[576,576]{1,0:T(8,128)}, f32[576,576]{1,0:T(8,128)}, ...) | async-done | bytes 6635536 | tf_op jit(solution)/shard_map/psum | solution.py:39
  468.3 6.7 %bitcast_dynamic-update-slice_fusion.7 = (f32[5,576,576]{2,1,0:T(8,128)S(1)}, f32[576,576]{1,0:T(8,128)S(1)}) fusion(f32[576,576]{1,0:T(8,128)} %get-tuple-element.50, f32[576,576]{0,1:T(8,128)} %copy-done.9), kind=kOutput, calls=%fused_computation.11 | convolution fusion | flops 2293567488 | bytes 7372800 | tf_op jit(solution)/shard_map/dot_general | solution.py:10
  475.0 4.4 add_negate_fusion.1
  479.5 4.2 bitcast_dynamic-update-slice_fusion.6
  483.8 4.3 add_negate_fusion
  488.1 4.5 bitcast_dynamic-update-slice_fusion.5
  492.8 3.0 copy-done.31
  (169 shorter events, 81.7 us)
Async XLA Ops:
  7.2 254.2 %all-gather.12.cloned.1.call-start = ((), (), s32[]{:S(2)}) async-start(), calls=%async_computation.3 | async-start | bytes 1843200 | tf_op jit(solution)/shard_map/all_gather | solution.py:19
  7.9 260.7 %all-gather.6.cloned.1.call-start = ((), (), s32[]{:S(2)}) async-start(), calls=%async_computation | async-start | bytes 3317760 | tf_op jit(solution)/shard_map/all_gather | solution.py:34
  8.1 157.1 %copy-start.7 = (f32[576,576]{0,1:T(8,128)}, f32[576,576]{0,1:T(8,128)S(1)}, u32[]{:S(2)}) copy-start(f32[576,576]{0,1:T(8,128)S(1)} %fusion.6) | copy-start | bytes 3981316
  12.3 28.3 %copy-start.24 = (f32[576,576]{1,0:T(8,128)}, f32[576,576]{1,0:T(8,128)S(1)}, u32[]{:S(2)}) copy-start(f32[576,576]{1,0:T(8,128)S(1)} %get-tuple-element.185) | copy-start | bytes 3981316
  39.7 54.0 %copy-start.34 = (s32[1,3]{1,0:T(1,128)S(1)}, s32[1,3]{1,0:T(1,128)}, u32[]{:S(2)}) copy-start(s32[1,3]{1,0:T(1,128)} %param.11) | copy-start | bytes 40
  93.7 3.5 copy-start.32
  102.2 4.1 copy-start.9
  108.0 169.6 %all-gather.8.cloned.1.call-start = ((), (), s32[]{:S(2)}) async-start(), calls=%async_computation.1 | async-start | bytes 3317760 | tf_op jit(solution)/shard_map/all_gather | solution.py:34
  171.6 13.2 %copy-start.10 = (f32[576,288]{0,1:T(8,128)}, f32[576,288]{0,1:T(8,128)S(1)}, u32[]{:S(2)}) copy-start(f32[576,288]{0,1:T(8,128)S(1)} %convolution_select_fusion.1) | copy-start | bytes 1990660
  171.6 13.2 %copy-start.33 = (f32[1,128,128]{2,1,0:T(8,128)S(1)}, f32[1,128,128]{2,1,0:T(8,128)}, u32[]{:S(2)}) copy-start(f32[1,128,128]{2,1,0:T(8,128)} %get-tuple-element.66) | copy-start | bytes 196612
  172.5 124.0 %all-gather.10.cloned.1.call-start = ((), (), s32[]{:S(2)}) async-start(), calls=%async_computation.2 | async-start | bytes 3317760 | tf_op jit(solution)/shard_map/all_gather | solution.py:34
  234.0 3.3 copy-start.8
  249.0 219.3 %all-reduce.5.cloned.1.call-start = ((), (), s32[]{:S(2)}) async-start(), calls=%async_computation.4 | async-start | bytes 14745600 | tf_op jit(solution)/shard_map/psum | solution.py:39
  249.2 6.8 %copy-start.26 = (f32[1,2,576,576]{3,2,1,0:T(8,128)S(1)}, f32[1,2,576,576]{3,2,1,0:T(8,128)}, u32[]{:S(2)}) copy-start(f32[1,2,576,576]{3,2,1,0:T(8,128)} %param.10) | copy-start | bytes 7962628
  268.6 5.1 %copy-start.19 = (f32[576,288]{0,1:T(8,128)S(1)}, f32[576,288]{0,1:T(8,128)}, u32[]{:S(2)}) copy-start(f32[576,288]{0,1:T(8,128)} %copy-done.18) | copy-start | bytes 1990660
  277.7 3.7 copy-start.2
  277.7 3.7 copy-start.16
  284.4 8.2 %copy-start.4 = (f32[288,576]{1,0:T(8,128)}, f32[288,576]{1,0:T(8,128)S(1)}, u32[]{:S(2)}) copy-start(f32[288,576]{1,0:T(8,128)S(1)} %fusion.10) | copy-start | bytes 1990660
  284.4 3.9 copy-start.11
  296.5 3.6 copy-start
  296.5 3.6 copy-start.5
  312.6 5.3 %copy-start.6 = (f32[288,576]{1,0:T(8,128)S(1)}, f32[288,576]{1,0:T(8,128)}, u32[]{:S(2)}) copy-start(f32[288,576]{1,0:T(8,128)} %copy-done.4) | copy-start | bytes 1990660
  312.6 5.3 %copy-start.17 = (f32[576,288]{0,1:T(8,128)S(1)}, f32[576,288]{0,1:T(8,128)}, u32[]{:S(2)}) copy-start(f32[576,288]{0,1:T(8,128)} %copy-done.15) | copy-start | bytes 1990660
  312.6 5.3 %copy-start.21 = (f32[288,576]{1,0:T(8,128)S(1)}, f32[288,576]{1,0:T(8,128)}, u32[]{:S(2)}) copy-start(f32[288,576]{1,0:T(8,128)} %copy-done.20) | copy-start | bytes 1990660
  468.3 6.7 %copy-start.3 = (f32[576,576]{1,0:T(8,128)S(1)}, f32[576,576]{1,0:T(8,128)}, u32[]{:S(2)}) copy-start(f32[576,576]{1,0:T(8,128)} %fusion.2) | copy-start | bytes 3981316
  468.3 6.7 %copy-start.30 = (f32[576,576]{1,0:T(8,128)S(1)}, f32[576,576]{1,0:T(8,128)}, u32[]{:S(2)}) copy-start(f32[576,576]{1,0:T(8,128)} %get-tuple-element.52) | copy-start | bytes 3981316
  475.0 4.5 copy-start.23
  475.0 4.5 copy-start.29
  479.5 4.2 copy-start.1
  479.5 4.2 copy-start.28
  483.8 4.3 copy-start.22
  483.8 4.3 copy-start.27
  (8 other events, 14.0 us)
Sparse Core Ops, SparseCore 0:
  9.8 32.9 all-gather.11
  108.2 39.4 all-gather.5
  172.6 39.3 all-gather.7
  249.1 39.3 all-gather.9
  307.3 160.9 all-reduce.4
where the time goes:
time: 512 us; the launch traced here: 503 us
  other arithmetic  162 us (32%)
  waiting for transfers between devices  150 us (29%)
  matrix products  124 us (24%)
  local copies, waits for them, and re-layouts  51.7 us (10%)
  between operations  15.1 us (3%)
    another operation x10, other arithmetic, on_device(): jax.scipy.linalg.solve_triangular(diag_factor[0, layer_index], identity,...  156 us
    psum x1, waiting for transfers between devices, on_device(): block = gram - lax.psum(product(scaled.T, panel), 'row')  149 us
    dot_general x19, matrix products, product(): jnp.dot(left_mat, right_mat, precision=HIGHEST, preferred_element_type=jn...  83.7 us
    another operation x43, local copies, waits for them, and re-layouts, on_device(): jax.scipy.linalg.solve_triangular(diag_factor[0, layer_index], identity,...  37 us
    another operation x27, matrix products, on_device(): jax.scipy.linalg.solve_triangular(diag_factor[0, layer_index], identity,...  28.5 us
    dot_general x3, matrix products, on_device(): jnp.dot(root_rows, lax.all_gather(scaled.astype(jnp.bfloat16), 'row', axi...  11.5 us
    unnamed x72, local copies, waits for them, and re-layouts  11.3 us
  transfers between devices with their start and end apart: 5, of which 1 were waited for; matrix products, arithmetic and copies ran while one was open for 59% of the time, Pallas kernels for 0%

commit v1 on v0

v1 whole, which is shorter than its diff:
```python
import functools
import jax
import jax.numpy as jnp
from jax import lax
from jax.experimental import pallas as pl
from jax.experimental.pallas import tpu as pltpu
from jax.sharding import PartitionSpec as P

BF = jnp.bfloat16
F32 = jnp.float32


def product(left_mat, right_mat):
    return jnp.dot(left_mat, right_mat, precision=lax.Precision.HIGH, preferred_element_type=F32)


def split(x):
    hi = x.astype(BF)
    return hi, (x - hi.astype(F32)).astype(BF)


def mm(a, b):
    return jnp.dot(a, b, preferred_element_type=F32)


def dot3(a, b):
    a_hi, a_lo = a
    b_hi, b_lo = b
    return mm(a_hi, b_hi) + (mm(a_lo, b_hi) + mm(a_hi, b_lo))


def inverse_kernel(size, window, l_ref, out_ref):
    count = size // window
    row = lax.broadcasted_iota(jnp.int32, (window, window), 0)
    col = lax.broadcasted_iota(jnp.int32, (window, window), 1)
    eye = row == col
    diagonals = []
    for w in range(count):
        at = slice(w * window, (w + 1) * window)
        block = l_ref[0, 0, at, at]
        kept = jnp.where(eye, block, 0.0)
        down = 1.0 / jnp.sum(kept, axis=1, keepdims=True)
        across = 1.0 / jnp.sum(kept, axis=0, keepdims=True)
        diagonals.append((block * down, across))
    found = []
    for scaled, across in diagonals:
        x = jnp.where(eye, 1.0, 0.0)
        x = x - jnp.where((row // 2 == col // 2) & (row > col), scaled, 0.0)
        found.append(x)
    k = 2
    while k < window:
        pair = (row // (2 * k) == col // (2 * k)) & (row // k > col // k)
        for w in range(count):
            x = found[w]
            parts = split(x)
            right = dot3(split(jnp.where(pair, diagonals[w][0], 0.0)), parts)
            found[w] = x - dot3(parts, split(right))
        k *= 2
    found = [x * diagonals[w][1] for w, x in enumerate(found)]
    done = {}
    for w in range(count):
        done[w, w] = split(found[w])
        out_ref[0, w * window:(w + 1) * window, w * window:(w + 1) * window] = found[w]
    for gap in range(1, count):
        for c in range(count - gap):
            r = c + gap
            total = None
            for m in range(c, r):
                below = split(l_ref[0, 0, r * window:(r + 1) * window, m * window:(m + 1) * window])
                term = dot3(below, done[m, c])
                total = term if total is None else total + term
            value = -dot3(done[r, r], split(total))
            done[r, c] = split(value)
            out_ref[0, r * window:(r + 1) * window, c * window:(c + 1) * window] = value
            out_ref[0, c * window:(c + 1) * window, r * window:(r + 1) * window] = jnp.zeros(
                (window, window), F32
            )


def inverses(diag_factor):
    levels, size = diag_factor.shape[1], diag_factor.shape[-1]
    return pl.pallas_call(
        functools.partial(inverse_kernel, size, size // 3),
        grid=(levels,),
        in_specs=[pl.BlockSpec((1, 1, size, size), lambda i: (0, i, 0, 0))],
        out_specs=pl.BlockSpec((1, size, size), lambda i: (i, 0, 0)),
        out_shape=jax.ShapeDtypeStruct((levels, size, size), F32),
        compiler_params=pltpu.CompilerParams(vmem_limit_bytes=48 * 2**20),
        name="inverses",
    )(diag_factor)


def on_device(root_cov, diag_factor, panel_factor, chain_factor, panel_tiles):
    node_width = diag_factor.shape[-1]
    rows_here = panel_factor.shape[2]
    per_tile = node_width // rows_here
    row_count = lax.axis_size("row")
    tile_total = row_count // per_tile
    counts = (3 * tile_total // 4, tile_total // 2, tile_total // 4)
    root_rows = lax.all_gather(root_cov, "branch", axis=1, tiled=True)
    me = lax.axis_index("row")
    my_tile = me // per_tile
    inverse_all = inverses(diag_factor)
    share = -(-node_width // row_count // 8) * 8
    padded = jnp.pad(inverse_all, ((0, 0), (0, share * row_count - node_width), (0, 0)))
    mine = lax.dynamic_slice_in_dim(padded, me * share, share, axis=1)
    chosen = [jnp.any(panel_tiles[0, : counts[i]] == my_tile) for i in range(3)]
    scaled = [
        jnp.where(chosen[i], product(panel_factor[0, i], inverse_all[i]), 0.0) for i in range(3)
    ]
    panels = []
    blocks = []
    crosses = []
    for i in range(3):
        gathered = jnp.dot(
            root_rows,
            lax.all_gather(scaled[i].astype(BF), "row", axis=0, tiled=True),
            preferred_element_type=F32,
        )
        left = jnp.concatenate([mine[i], scaled[i]], axis=0)
        if i == 0:
            panel = -jnp.where(chosen[i], gathered, 0.0)
            block = product(left.T, jnp.concatenate([mine[i], -panel], axis=0))
        else:
            chain = product(chain_factor[0, i - 1], inverse_all[i])
            panel = -jnp.where(chosen[i], gathered + product(panels[-1], chain), 0.0)
            cross = -(product(panels[-1].T, scaled[i]) + product(blocks[-1], chain))
            block = product(left.T, jnp.concatenate([mine[i], -panel], axis=0)) - product(
                chain.T, cross
            )
            crosses.append(cross)
        panels.append(panel)
        blocks.append(block)
    total = lax.psum(jnp.stack(blocks + crosses), "row")
    return (jnp.stack(panels)[None], total[None])


def solution(mesh):
    in_specs = (
        P("row", "branch"),
        P("branch", None, None, None),
        P("branch", None, "row", None),
        P("branch", None, None, None),
        P("branch", None),
    )
    out_specs = (P("branch", None, "row", None), P("branch", None, None, None))
    return jax.shard_map(
        on_device, mesh=mesh, in_specs=in_specs, out_specs=out_specs, check_vma=False
    )
```

time: 512 us -> 352 us (0.69)
  other arithmetic: 162 us -> 2.99 us
  waiting for transfers between devices: 150 us -> 230 us
  matrix products: 124 us -> 56.7 us
  local copies, waits for them, and re-layouts: 51.7 us -> 23 us
  Pallas kernels: 0 us -> 17 us
    another operation x10 -> x2, other arithmetic: 156 us -> 0.15 us  [on_device(): return (jnp.stack(panels)[None], total[None])]
    all_gather x3, waiting for transfers between devices: 0.02 us -> 77.7 us  [on_device(): lax.all_gather(scaled[i].astype(BF), 'row', axis=0, tiled=True)]
    dot_general x22 -> x19, matrix products: 95.1 us -> 56.7 us  [the longest x16 44.7 us: product(): jnp.dot(left_mat, right_mat, precision=lax.Precision.HIGH, preferred_elem...]
    another operation x44 -> x1, local copies, waits for them, and re-layouts: 37.1 us -> 0.1 us  [on_device(): total = lax.psum(jnp.stack(blocks + crosses), 'row')]
    another operation x27 -> x0, matrix products: 28.5 us -> none  [on_device(): jax.scipy.linalg.solve_triangular(diag_factor[0, layer_index], identity,...]
    pallas_call x0 -> x1, Pallas kernels: none -> 17 us  [inverses(): pl.pallas_call(functools.partial(inverse_kernel, size, size // 3), grid=(...]
    unnamed x72 -> x39, local copies, waits for them, and re-layouts: 11.3 us -> 18.5 us
  transfers between devices with their start and end apart: 5 -> 5, of which waited for: 1 -> 4; matrix products, arithmetic and copies ran while one was open for 59% -> 15% of each run, Pallas kernels for 0% -> 5%
where the time goes in v1:
time: 352 us; the launch traced here: 345 us
  waiting for transfers between devices  230 us (65%)
  matrix products  56.7 us (16%)
  local copies, waits for them, and re-layouts  23 us (7%)
  Pallas kernels  17 us (5%)
  between operations  14.6 us (4%)
    psum x1, waiting for transfers between devices, on_device(): total = lax.psum(jnp.stack(blocks + crosses), 'row')  152 us
    all_gather x3, waiting for transfers between devices, on_device(): lax.all_gather(scaled[i].astype(BF), 'row', axis=0, tiled=True)  77.7 us
    dot_general x16, matrix products, product(): jnp.dot(left_mat, right_mat, precision=lax.Precision.HIGH, preferred_elem...  44.7 us
    unnamed x39, local copies, waits for them, and re-layouts  18.5 us
    pallas_call x1, Pallas kernels, inverses(): pl.pallas_call(functools.partial(inverse_kernel, size, size // 3), grid=(...  17 us
    dot_general x3, matrix products, on_device(): jnp.dot(root_rows, lax.all_gather(scaled[i].astype(BF), 'row', axis=0, ti...  12 us
  transfers between devices with their start and end apart: 5, of which 4 were waited for; matrix products, arithmetic and copies ran while one was open for 15% of the time, Pallas kernels for 5%

profile of v1, /device:TPU:0, one launch (start us, length us, event | category | flops | bytes accessed | tf_op | source)
XLA Modules:
  0.0 344.9 jit_solution(14881078782614802303)
XLA Ops:
  8.0 17.0 %inverses.1 = f32[3,576,576]{2,1,0:T(8,128)S(1)} custom-call(f32[1,3,576,576]{3,2,1,0:T(8,128)} %l_ref.1), custom_call_target="tpu_custom_call" | custom-call | tf_op jit(solution)/shard_map/inverses/pallas_call | solution.py:82
  25.0 2.1 copy-done
  27.8 4.2 %fusion.38 = (bf16[288,576]{1,0:T(8,128)(2,1)}, f32[288,576]{1,0:T(8,128)}) fusion(f32[3,576,576]{2,1,0:T(8,128)} %copy-done, f32[1,3,288,576]{3,2,1,0:T(8,128)S(1)} %copy-done.15, pred[]{:T(512)} %compare_reduce_fusion), kind=kOutput, calls=%fused_computation.69 | convolution fusion | flops 573640704 | bytes 3207680 | tf_op jit(solution)/shard_map/dot_general | solution.py:14
  32.7 4.2 %fusion.39 = (bf16[288,576]{1,0:T(8,128)(2,1)}, f32[288,576]{1,0:T(8,128)}) fusion(f32[3,576,576]{2,1,0:T(8,128)} %copy-done, f32[1,3,288,576]{3,2,1,0:T(8,128)S(1)} %copy-done.15, pred[]{:T(512)} %compare_reduce_fusion.1), kind=kOutput, calls=%fused_computation.70 | convolution fusion | flops 573640704 | bytes 3207680 | tf_op jit(solution)/shard_map/dot_general | solution.py:14
  37.0 3.6 %fusion.37 = (bf16[288,576]{1,0:T(8,128)(2,1)}, f32[288,576]{1,0:T(8,128)}) fusion(f32[3,576,576]{2,1,0:T(8,128)} %copy-done, f32[1,3,288,576]{3,2,1,0:T(8,128)S(1)} %copy-done.15, pred[]{:T(512)} %bitcast.13), kind=kOutput, calls=%fused_computation.68 | convolution fusion | flops 573640704 | bytes 3207680 | tf_op jit(solution)/shard_map/dot_general | solution.py:14
  40.8 1.1 dynamic-slice_bitcast_fusion
  42.0 4.1 %fusion.1 = f32[576,576]{1,0:T(8,128)S(1)} fusion(f32[1,2,576,576]{3,2,1,0:T(8,128)} %param.8, f32[3,576,576]{2,1,0:T(8,128)} %copy-done), kind=kOutput, calls=%fused_computation.10 | convolution fusion | flops 1146617856 | bytes 4276224 | tf_op jit(solution)/shard_map/dot_general | solution.py:14
  46.1 3.5 %fusion.3 = f32[576,576]{1,0:T(8,128)S(1)} fusion(f32[1,2,576,576]{3,2,1,0:T(8,128)S(1)} %copy-done.14, f32[3,576,576]{2,1,0:T(8,128)} %copy-done), kind=kOutput, calls=%fused_computation.12 | convolution fusion | flops 1146617856 | bytes 4276224 | tf_op jit(solution)/shard_map/dot_general | solution.py:14
  49.6 3.3 copy.8
  52.9 4.1 %reshape.10 = bf16[2304,288]{0,1:T(8,128)(2,1)} reshape(bf16[4,576,288]{1,0,2:T(4,128)(2,1)} %copy.8) | data formatting | bytes 2654208
  57.0 24.1 %all-gather.8.cloned.1.call-done = bf16[2304,576]{1,0:T(8,128)(2,1)} async-done(((bf16[288,576]{1,0:T(8,128)(2,1)}), bf16[2304,576]{1,0:T(8,128)(2,1)}) %all-gather.8.cloned.1.call-update) | async-done | bytes 2654224 | tf_op jit(solution)/shard_map/all_gather | solution.py:117
  81.1 4.3 %convolution_bitcast_fusion.1 = f32[288,576]{1,0:T(8,128)} fusion(bf16[2304,288]{0,1:T(8,128)(2,1)} %reshape.10, bf16[2304,576]{1,0:T(8,128)(2,1)} %all-gather.8.cloned.1.call-done), kind=kOutput, calls=%fused_computation.25 | convolution fusion | flops 764411904 | bytes 4644864 | tf_op jit(solution)/shard_map/dot_general | solution.py:115
  85.4 32.9 %all-gather.6.cloned.1.call-done = bf16[2304,576]{1,0:T(8,128)(2,1)} async-done(((bf16[288,576]{1,0:T(8,128)(2,1)}), bf16[2304,576]{1,0:T(8,128)(2,1)}) %all-gather.6.cloned.1.call-update) | async-done | bytes 2654224 | tf_op jit(solution)/shard_map/all_gather | solution.py:117
  118.3 4.1 %fusion.14 = f32[288,576]{1,0:T(8,128)S(1)} fusion(bf16[2304,288]{0,1:T(8,128)(2,1)} %reshape.10, bf16[2304,576]{1,0:T(8,128)(2,1)} %all-gather.6.cloned.1.call-done, pred[]{:T(512)} %compare_reduce_fusion.1), kind=kOutput, calls=%fused_computation.31 | convolution fusion | flops 764577792 | bytes 4644865 | tf_op jit(solution)/shard_map/dot_general | solution.py:115
  122.5 1.9 fusion.13
  124.4 2.7 fusion.16
  127.1 2.7 bitcast_dynamic-update-slice_fusion.4
  129.8 2.2 fusion.40
  132.0 2.7 add_negate_fusion.1
  134.7 20.6 %all-gather.10.cloned.1.call-done = bf16[2304,576]{1,0:T(8,128)(2,1)} async-done(((bf16[288,576]{1,0:T(8,128)(2,1)}), bf16[2304,576]{1,0:T(8,128)(2,1)}) %all-gather.10.cloned.1.call-update) | async-done | bytes 2654224 | tf_op jit(solution)/shard_map/all_gather | solution.py:117
  155.4 3.6 %convolution_bitcast_fusion = f32[288,576]{1,0:T(8,128)S(1)} fusion(bf16[2304,288]{0,1:T(8,128)(2,1)} %reshape.10, bf16[2304,576]{1,0:T(8,128)(2,1)} %all-gather.10.cloned.1.call-done), kind=kOutput, calls=%fused_computation.24 | convolution fusion | flops 764411904 | bytes 4644864 | tf_op jit(solution)/shard_map/dot_general | solution.py:115
  159.0 1.5 fusion.12
  160.6 3.8 %bitcast_dynamic-update-slice_fusion.3 = (f32[5,576,576]{2,1,0:T(8,128)S(1)}, f32[576,576]{1,0:T(8,128)S(1)}) fusion(f32[5,576,576]{2,1,0:T(8,128)S(1)} %copy-done.7, f32[576,576]{1,0:T(8,128)} %fusion.16, f32[576,576]{1,0:T(8,128)S(1)} %fusion.3, f32[576,576]{1,0:T(8,128)S(1)} %copy-done.4), kind=kOutput, calls=%fused_computation.8 | convolution fusion | flops 1146949632 | bytes 7225344 | tf_op jit(solution)/shard_map/dot_general | solution.py:14
  164.4 2.2 fusion.41
  166.6 1.6 add_negate_fusion
  168.2 1.6 fusion.15
  169.8 2.3 bitcast_dynamic-update-slice_fusion.2
  172.3 3.0 copy-done.8
  175.4 1.1 copy-done.6
  177.9 1.5 maximum_bitcast_fusion
  179.4 151.9 %all-reduce.2.cloned.1.call-done = f32[1,5,576,576]{3,2,1,0:T(8,128)} async-done(((f32[1,5,576,576]{3,2,1,0:T(8,128)}), f32[1,5,576,576]{3,2,1,0:T(8,128)}) %all-reduce.2.cloned.1.call-update) | async-done | bytes 6635536 | tf_op jit(solution)/shard_map/psum | solution.py:134
  331.3 6.6 %copy.14 = f32[1,5,576,576]{3,2,1,0:T(8,128)} copy(f32[1,5,576,576]{3,2,1,0:T(8,128)} %all-reduce.2.cloned.1.call-done) | data formatting | bytes 13271040
  (50 shorter events, 4.3 us)
Async XLA Ops:
  7.2 42.5 %all-gather.12.cloned.1.call-start = ((), (), s32[]{:S(2)}) async-start(), calls=%async_computation.4 | async-start | bytes 1843200 | tf_op jit(solution)/shard_map/all_gather | solution.py:100
  7.9 73.2 %all-gather.8.cloned.1.call-start = ((), (), s32[]{:S(2)}) async-start(), calls=%async_computation.1 | async-start | bytes 3317760 | tf_op jit(solution)/shard_map/all_gather | solution.py:117
  8.0 19.1 %copy-start.17 = (s32[1,3]{1,0:T(1,128)S(1)}, s32[1,3]{1,0:T(1,128)}, u32[]{:S(2)}) copy-start(s32[1,3]{1,0:T(1,128)} %param.9) | copy-start | bytes 40
  8.0 19.8 %copy-start.15 = (f32[1,3,288,576]{3,2,1,0:T(8,128)S(1)}, f32[1,3,288,576]{3,2,1,0:T(8,128)}, u32[]{:S(2)}) copy-start(f32[1,3,288,576]{3,2,1,0:T(8,128)} %param.7) | copy-start | bytes 5971972
  25.0 2.1 copy-start
  32.0 86.3 %all-gather.6.cloned.1.call-start = ((), (), s32[]{:S(2)}) async-start(), calls=%async_computation | async-start | bytes 3317760 | tf_op jit(solution)/shard_map/all_gather | solution.py:117
  36.9 118.5 %all-gather.10.cloned.1.call-start = ((), (), s32[]{:S(2)}) async-start(), calls=%async_computation.2 | async-start | bytes 3317760 | tf_op jit(solution)/shard_map/all_gather | solution.py:117
  40.6 290.7 %all-reduce.2.cloned.1.call-start = ((), (), s32[]{:S(2)}) async-start(), calls=%async_computation.3 | async-start | bytes 14745600 | tf_op jit(solution)/shard_map/psum | solution.py:134
  42.0 4.1 %copy-start.14 = (f32[1,2,576,576]{3,2,1,0:T(8,128)S(1)}, f32[1,2,576,576]{3,2,1,0:T(8,128)}, u32[]{:S(2)}) copy-start(f32[1,2,576,576]{3,2,1,0:T(8,128)} %param.8) | copy-start | bytes 7962628
  118.3 4.2 %copy-start.16 = (f32[288,576]{1,0:T(8,128)S(1)}, f32[288,576]{1,0:T(8,128)}, u32[]{:S(2)}) copy-start(f32[288,576]{1,0:T(8,128)} %convolution_bitcast_fusion.1) | copy-start | bytes 1990660
  122.5 9.5 %copy-start.5 = (f32[288,576]{1,0:T(8,128)}, f32[288,576]{1,0:T(8,128)S(1)}, u32[]{:S(2)}) copy-start(f32[288,576]{1,0:T(8,128)S(1)} %fusion.14) | copy-start | bytes 1990660
  122.5 1.9 copy-start.9
  124.4 2.7 copy-start.1
  124.4 2.7 copy-start.13
  155.4 3.6 %copy-start.2 = (f32[288,576]{1,0:T(8,128)S(1)}, f32[288,576]{1,0:T(8,128)}, u32[]{:S(2)}) copy-start(f32[288,576]{1,0:T(8,128)} %copy-done.1) | copy-start | bytes 1990660
  155.4 5.1 %copy-start.7 = (f32[5,576,576]{2,1,0:T(8,128)S(1)}, f32[5,576,576]{2,1,0:T(8,128)}, u32[]{:S(2)}) copy-start(f32[5,576,576]{2,1,0:T(8,128)} %get-tuple-element.11) | copy-start | bytes 19906564
  159.0 1.6 copy-start.4
  160.4 7.7 %copy-start.11 = (f32[288,576]{1,0:T(8,128)}, f32[288,576]{1,0:T(8,128)S(1)}, u32[]{:S(2)}) copy-start(f32[288,576]{1,0:T(8,128)S(1)} %fusion.12) | copy-start | bytes 1990660
  164.4 2.2 copy-start.10
  172.3 3.1 copy-start.8
  175.4 1.1 copy-start.6
  176.5 1.1 copy-start.3
  176.5 1.3 copy-start.12
Sparse Core Ops, SparseCore 0:
  9.8 32.8 all-gather.11
  44.4 36.6 all-gather.7
  82.7 35.5 all-gather.5
  119.8 35.5 all-gather.9
  175.5 155.7 all-reduce.1
